TPU v7x, 32 devices: a whole 2x2x4 slice. The times are simulated.
32 devices in a mesh: tm: 32 (over z, y, x, core).
Axes of the slice: x: 2, y: 2, z: 4, core: 2. Of those that a mesh axis runs over, the one named last changes fastest.
Arguments:
- transition: float32 [256, 256], replicated, may hold values from -1 to 1
- noise_var: float32 [256], replicated, may hold values from 0.001 to 0.1
- prior_mean: float32 [256], replicated, may hold values from -6 to 6
- prior_var: float32 [256], replicated, may hold values from 0.5 to 2
- obs_op: bfloat16 [32, 8, 128, 128], P('tm'), may hold values from -0.5 to 0.5
- obs_value: float32 [32, 8, 128], P('tm'), may hold values from -18 to 18
- obs_noise: float32 [32, 8, 128], P('tm'), may hold values from 10 to 100
- obs_block: int32 [32, 8], P('tm'), may hold values from 0 to 1
- obs_count: int32 [32], P('tm'), may hold values from 1 to 8, as said below
Outputs:
- smoothed_mean: float32 [32, 256], P('tm')
- smoothed_var: float32 [32, 256], P('tm')
Inputs may be any that keep to these rules, and one draw needn't show every extreme that they name: Only the first obs_count[t] slots of step t carry observations; some step reports all 8.
All inputs are finite; a program needn't handle non-finite values.
Results may differ from a plain program's by a relative error of at most 0.024.
Values sent between devices are 32-bit elements; how exact they have to be, the bound alone decides.
A program may use at most 192 MiB of HBM per device.

v0:
```python
import jax
import jax.numpy as jnp
from jax import lax
from jax.sharding import PartitionSpec as P

precise = lax.Precision.HIGHEST


def passed_along(value, axis, steps):
    count = lax.axis_size(axis)
    first, last = (max(0, -steps), min(count, count - steps))
    return lax.ppermute(value, axis, [(source, source + steps) for source in range(first, last)])


def product(left, right):
    return jnp.dot(left, right, precision=precise, preferred_element_type=jnp.float32)


def woodbury_parts(covariance, info_matrix):
    size = covariance.shape[0]
    factor = jnp.linalg.cholesky(covariance)
    cross = product(factor.T, info_matrix)
    inner = jnp.eye(size, dtype=jnp.float32) + product(cross, factor)
    inner_factor = jnp.linalg.cholesky(inner)
    left_part = jax.scipy.linalg.solve_triangular(inner_factor, factor.T, lower=True).T
    right_part = jax.scipy.linalg.solve_triangular(inner_factor, cross, lower=True)
    return (left_part, right_part)


def fold_real(earlier, later):
    lin_early, off_early, cov_early, vec_early, inf_early = earlier[1:]
    lin_late, off_late, cov_late, vec_late, inf_late = later[1:]
    size = cov_early.shape[0]
    left_part, right_part = woodbury_parts(cov_early, inf_late)
    weight = jnp.eye(size, dtype=jnp.float32) - product(left_part, right_part)
    damped_cov = product(left_part, left_part.T)
    damped_info = inf_late - product(right_part.T, right_part)
    lin_weight = product(lin_late, weight)
    linear = product(lin_weight, lin_early)
    offset = (
        product(lin_weight, off_early) + product(lin_late, product(damped_cov, vec_late)) + off_late
    )
    covariance = product(product(lin_late, damped_cov), lin_late.T) + cov_late
    moved = vec_late - product(inf_late, off_early)
    pulled = moved - product(right_part.T, product(left_part.T, moved))
    info_vector = product(lin_early.T, pulled) + vec_early
    info_matrix = product(product(lin_early.T, damped_info), lin_early) + inf_early
    return (linear, offset, covariance, info_vector, info_matrix)


def fold_filter(earlier, later):
    present = jnp.maximum(earlier[0], later[0])

    def joined():
        return (present,) + fold_real(earlier, later)

    def passed():
        return tuple(
            (
                jnp.where(earlier[0] > 0, first_part, second_part)
                for first_part, second_part in zip(earlier, later)
            )
        )

    return lax.cond(earlier[0] * later[0] > 0, joined, passed)


def fold_smooth(higher, lower):
    gain_high, shift_high, spread_high = higher
    gain_low, shift_low, spread_low = lower
    gain = product(gain_low, gain_high)
    shift = product(gain_low, shift_high) + shift_low
    spread = product(product(gain_low, spread_high), gain_low.T) + spread_low
    return (gain, shift, spread)


def select_parts(valid, first_parts, second_parts):
    return tuple(
        (
            jnp.where(valid, first_part, second_part)
            for first_part, second_part in zip(first_parts, second_parts)
        )
    )


def build_element(step_index, info_dense, info_shift, transition, noise_var, prior_mean, prior_var):
    size = transition.shape[0]
    eye = jnp.eye(size, dtype=jnp.float32)
    first = step_index == 0
    prec_diag = jnp.where(first, 1.0 / prior_var, 1.0 / noise_var)
    prior_term = jnp.where(first, prior_mean / prior_var, jnp.zeros_like(prior_mean))
    moving = jnp.where(first, jnp.zeros_like(transition), transition)
    factor = jnp.linalg.cholesky(jnp.diag(prec_diag) + info_dense)
    covariance = jax.scipy.linalg.cho_solve((factor, True), eye)
    linear = product(covariance * prec_diag[None, :], moving)
    offset = product(covariance, prior_term + info_shift)
    gain_cov = product(info_dense, covariance)
    info_vector = product(moving.T, info_shift - product(gain_cov, info_shift))
    info_matrix = product(product(moving.T, info_dense - product(gain_cov, info_dense)), moving)
    return (jnp.ones((), jnp.float32), linear, offset, covariance, info_vector, info_matrix)


def local(
    transition, noise_var, prior_mean, prior_var, obs_op, obs_value, obs_noise, obs_block, obs_count
):
    steps, slots, stations, width = obs_op.shape
    size = transition.shape[0]
    nblocks = size // width
    eye = jnp.eye(size, dtype=jnp.float32)
    zero_vec = jnp.zeros((size,), jnp.float32)
    zero_mat = jnp.zeros((size, size), jnp.float32)
    active = (lax.broadcasted_iota(jnp.int32, (steps, slots), 1) < obs_count[:, None]).astype(
        jnp.float32
    )
    block_ids = lax.broadcasted_iota(jnp.int32, (steps, slots, nblocks), 2)
    chosen = (obs_block[:, :, None] == block_ids).astype(jnp.float32) * active[:, :, None]
    scaled = (obs_op.astype(jnp.float32) / obs_noise[:, :, :, None]).astype(jnp.bfloat16)
    weighted = obs_value / obs_noise
    slot_info = jnp.einsum("kmsi,kmsj->kmij", scaled, obs_op, preferred_element_type=jnp.float32)
    slot_shift = jnp.einsum(
        "kmsi,kms->kmi", obs_op.astype(jnp.float32), weighted, precision=precise
    )
    block_info = jnp.einsum("kmn,kmij->knij", chosen, slot_info, precision=precise)
    block_shift = jnp.einsum("kmn,kmi->kni", chosen, slot_shift, precision=precise)
    info_dense = jnp.einsum(
        "knij,nc->knicj", block_info, jnp.eye(nblocks, dtype=jnp.float32), precision=precise
    ).reshape(steps, size, size)
    shift_all = block_shift.reshape(steps, size)
    device = lax.axis_index("tm")
    devices = lax.axis_size("tm")
    offsets = [1] + [1 << level for level in range((devices - 1).bit_length())]
    step_index = device * steps + jnp.arange(steps, dtype=jnp.int32)
    total_steps = steps * devices
    elements = jax.vmap(build_element, in_axes=(0, 0, 0, None, None, None, None))(
        step_index, info_dense, shift_all, transition, noise_var, prior_mean, prior_var
    )
    head = tuple((part[0] for part in elements))
    rest = tuple((part[1:] for part in elements))

    def forward_step(carry, item):
        joined = fold_filter(carry, item)
        return (joined, joined)

    aggregate, tail = lax.scan(forward_step, head, rest)
    prefixes = tuple(
        (
            jnp.concatenate([first_part[None], later_part], axis=0)
            for first_part, later_part in zip(head, tail)
        )
    )
    identity = (jnp.zeros((), jnp.float32), eye, zero_vec, zero_mat, zero_vec, zero_mat)
    entering = aggregate
    for turn, offset in enumerate(offsets):
        received = passed_along(entering, "tm", offset)
        valid = device >= offset
        if turn == 0:
            entering = select_parts(valid, received, identity)
        else:
            entering = select_parts(valid, fold_filter(received, entering), entering)

    def filtered_state(prefix):

        def joined():
            left_part, right_part = woodbury_parts(entering[3], prefix[5])
            damped_cov = product(left_part, left_part.T)
            start = entering[2]
            passed_mean = (
                start
                - product(left_part, product(right_part, start))
                + product(damped_cov, prefix[4])
            )
            mean = product(prefix[1], passed_mean) + prefix[2]
            cov = product(product(prefix[1], damped_cov), prefix[1].T) + prefix[3]
            return (mean, cov)

        def alone():
            return (prefix[2], prefix[3])

        return lax.cond(entering[0] > 0, joined, alone)

    means, covs = lax.map(filtered_state, prefixes)

    def smooth_element(index, mean, cov):
        moved = product(transition, cov)
        predicted = product(moved, transition.T) + jnp.diag(noise_var)
        factor = jnp.linalg.cholesky(predicted)
        gain = jax.scipy.linalg.cho_solve((factor, True), moved).T
        gain = jnp.where(index == total_steps - 1, jnp.zeros_like(gain), gain)
        shift = mean - product(gain, product(transition, mean))
        spread = cov - product(gain, moved)
        return (gain, shift, spread)

    gains, shifts, spreads = jax.vmap(smooth_element)(step_index, means, covs)

    def backward_step(carry, item):
        joined = fold_smooth(carry, item)
        return (joined, joined)

    lowest, lower = lax.scan(
        backward_step,
        (gains[-1], shifts[-1], spreads[-1]),
        (gains[:-1], shifts[:-1], spreads[:-1]),
        reverse=True,
    )
    suffixes = (
        jnp.concatenate([lower[0], gains[-1][None]], axis=0),
        jnp.concatenate([lower[1], shifts[-1][None]], axis=0),
        jnp.concatenate([lower[2], spreads[-1][None]], axis=0),
    )
    after = lowest
    for turn, offset in enumerate(offsets):
        received = passed_along(after, "tm", -offset)
        valid = device + offset < devices
        if turn == 0:
            after = select_parts(valid, received, (eye, zero_vec, zero_mat))
        else:
            after = select_parts(valid, fold_smooth(received, after), after)

    def finish(gain, shift, spread):
        mean = product(gain, after[1]) + shift
        variance = jnp.sum(product(gain, after[2]) * gain, axis=1) + jnp.diagonal(spread)
        return (mean, variance)

    smoothed_mean, smoothed_var = jax.vmap(finish)(suffixes[0], suffixes[1], suffixes[2])
    return (smoothed_mean, smoothed_var)


def solution(mesh):
    return jax.shard_map(
        local,
        mesh=mesh,
        in_specs=(
            P(),
            P(),
            P(),
            P(),
            P("tm", None, None, None),
            P("tm", None, None),
            P("tm", None, None),
            P("tm", None),
            P("tm"),
        ),
        out_specs=(P("tm", None), P("tm", None)),
        check_vma=False,
    )
```

profile of v0, /device:TPU:0, one launch (start us, length us, event | category | flops | bytes accessed | tf_op | source)
XLA Modules:
  0.0 1039.1 jit_solution(5291920049652089491)
XLA Ops:
  4.9 11.7 %custom-call.80 = f32[1,128,128]{2,1,0:T(8,128)S(1)} custom-call(f32[1,128,128]{2,1,0:T(8,128)S(1)} %copy.135), custom_call_target="Cholesky" | custom-call | tf_op jit(solution)/shard_map/vmap(jit(cholesky))/cholesky | solution.py:93
  16.6 9.8 custom-call.81
  27.2 11.7 %custom-call.82 = f32[1,128,128]{2,1,0:T(8,128)S(1)} custom-call(f32[1,128,128]{2,1,0:T(8,128)S(1)} %copy.137), custom_call_target="Cholesky" | custom-call | tf_op jit(solution)/shard_map/vmap(jit(cholesky))/cholesky | solution.py:93
  45.5 19.7 %custom-call.84 = f32[1,2,128,128]{2,3,1,0:T(8,128)S(1)} custom-call(f32[1,2,128,128]{3,2,1,0:T(8,128)S(1)} %bitcast.903), custom_call_target="InvertDiagBlocksLowerTriangular" | custom-call | tf_op jit(solution)/shard_map/vmap(jit(_cho_solve))/triangular_solve/custom-call.6 | solution.py:94
  78.3 6.0 collective-permute-start.8
  113.3 13.9 %conditional.6 = (f32[]{:T(128)}, f32[256]{0:T(256)S(1)}, f32[256]{0:T(256)S(1)}, f32[256,256]{0,1:T(8,128)}, f32[256,256]{0,1:T(8,128)}, /*index=5*/f32[256,256]{0,1:T(8,128)S(1)}) conditional(s32[]{:T(128)} %convert_element_type.85, (f32[]{:T(128)}, f32[]{:T(128)}, f32[256,256]{0,1:T(8,128)S(1)}, f32[256,256]{0,1:T(8,128)S(1)}, f32[256]{0:T(256)S(1)}, ...), branch_computations={%region_4.8_spmd, %region_5.15_spmd} | conditional | flops 2625210112 | bytes 26656268 | solution.py:65
  127.3 110.5 %collective-permute-start.17 = (f32[256,256]{0,1:T(8,128)S(1)}, f32[256,256]{0,1:T(8,128)S(1)}, u32[]{:S(2)}, u32[]{:S(2)}) collective-permute-start(f32[256,256]{0,1:T(8,128)S(1)} %broadcast_select_fusion.34), channel_id=1, source_target_pairs={{0,2},{1,3},{2,4},{3,5},{4,6},{5,7},{6,8},{7,9},{8,10},{9,11},{10,... | collective-permute-start | bytes 786440 | tf_op jit(solution)/shard_map/ppermute | solution.py:12
  259.5 16.0 %conditional.7 = (f32[]{:T(128)}, f32[256]{0:T(256)S(1)}, f32[256]{0:T(256)S(1)}, f32[256,256]{0,1:T(8,128)}, f32[256,256]{0,1:T(8,128)}, /*index=5*/f32[256,256]{0,1:T(8,128)}) conditional(s32[]{:T(128)} %convert_element_type.91, (f32[]{:T(128)}, f32[]{:T(128)}, f32[256,256]{0,1:T(8,128)S(1)}, f32[256,256]{0,1:T(8,128)S(1)}, f32[256]{0:T(256)S(1)}, ...), branch_computations={%region_10.16_spmd, %region_11.17_spmd} | conditional | flops 2625210112 | bytes 26648020 | solution.py:65
  275.6 108.7 %collective-permute-start.23 = (f32[256,256]{0,1:T(8,128)S(1)}, f32[256,256]{0,1:T(8,128)S(1)}, u32[]{:S(2)}, u32[]{:S(2)}) collective-permute-start(f32[256,256]{0,1:T(8,128)S(1)} %broadcast_select_fusion.31), channel_id=1, source_target_pairs={{0,4},{1,5},{2,6},{3,7},{4,8},{5,9},{6,10},{7,11},{8,12},{9,13},{1... | collective-permute-start | bytes 786440 | tf_op jit(solution)/shard_map/ppermute | solution.py:12
  384.4 5.7 collective-permute-start.21
  406.5 16.2 %conditional.8 = (f32[]{:T(128)}, f32[256]{0:T(256)S(1)}, f32[256]{0:T(256)S(1)}, f32[256,256]{0,1:T(8,128)}, f32[256,256]{0,1:T(8,128)}, /*index=5*/f32[256,256]{0,1:T(8,128)}) conditional(s32[]{:T(128)} %convert_element_type.92, (f32[]{:T(128)}, f32[]{:T(128)}, f32[256,256]{0,1:T(8,128)S(1)}, f32[256,256]{0,1:T(8,128)S(1)}, f32[256]{0:T(256)S(1)}, ...), branch_computations={%region_12.18_spmd, %region_13.19_spmd} | conditional | flops 2625210112 | bytes 26656268 | solution.py:65
  422.8 108.3 %collective-permute-start.29 = (f32[256,256]{0,1:T(8,128)S(1)}, f32[256,256]{0,1:T(8,128)S(1)}, u32[]{:S(2)}, u32[]{:S(2)}) collective-permute-start(f32[256,256]{0,1:T(8,128)S(1)} %broadcast_select_fusion.28), channel_id=1, source_target_pairs={{0,8},{1,9},{2,10},{3,11},{4,12},{5,13},{6,14},{7,15},{8,16},{9,17... | collective-permute-start | bytes 786440 | tf_op jit(solution)/shard_map/ppermute | solution.py:12
  550.1 12.9 %conditional.9 = (f32[]{:T(128)}, f32[256,256]{1,0:T(8,128)}, f32[256]{0:T(256)S(1)}, f32[256]{0:T(256)S(1)}, f32[256,256]{1,0:T(8,128)}, /*index=5*/f32[256,256]{0,1:T(8,128)S(1)}) conditional(s32[]{:T(128)} %convert_element_type.93, (f32[]{:T(128)}, f32[]{:T(128)}, f32[256,256]{0,1:T(8,128)S(1)}, f32[256,256]{0,1:T(8,128)S(1)}, ...), branch_computations={%region_14.20_spmd, %region_15.21_spmd} | conditional | flops 2625210112 | bytes 27172336 | solution.py:65
  563.0 108.3 %collective-permute-start.32 = (f32[256,256]{0,1:T(8,128)S(1)}, f32[256,256]{0,1:T(8,128)S(1)}, u32[]{:S(2)}, u32[]{:S(2)}) collective-permute-start(f32[256,256]{0,1:T(8,128)S(1)} %broadcast_select_fusion.27), channel_id=1, source_target_pairs={{0,16},{1,17},{2,18},{3,19},{4,20},{5,21},{6,22},{7,23},{8,24},{9,... | collective-permute-start | bytes 786440 | tf_op jit(solution)/shard_map/ppermute | solution.py:12
  677.1 10.2 conditional.10
  688.0 8.5 conditional.11
  697.8 11.7 %custom-call.85 = f32[1,128,128]{2,1,0:T(8,128)S(1)} custom-call(f32[1,128,128]{2,1,0:T(8,128)S(1)} %cholesky.1184), custom_call_target="Cholesky" | custom-call | tf_op jit(solution)/shard_map/vmap(jit(cholesky))/cholesky | solution.py:186
  709.5 9.8 custom-call.86
  719.8 11.7 %custom-call.87 = f32[1,128,128]{2,1,0:T(8,128)S(1)} custom-call(f32[1,128,128]{2,1,0:T(8,128)S(1)} %fusion.290), custom_call_target="Cholesky" | custom-call | tf_op jit(solution)/shard_map/vmap(jit(cholesky))/cholesky | solution.py:186
  739.0 19.7 %custom-call.89 = f32[1,2,128,128]{2,3,1,0:T(8,128)S(1)} custom-call(f32[1,2,128,128]{3,2,1,0:T(8,128)S(1)} %bitcast.902), custom_call_target="InvertDiagBlocksLowerTriangular" | custom-call | tf_op jit(solution)/shard_map/vmap(jit(_cho_solve))/triangular_solve/custom-call.6 | solution.py:187
  767.9 99.9 %collective-permute-done.38 = f32[256]{0:T(256)S(1)} collective-permute-done((f32[256]{0:T(256)S(1)}, f32[256]{0:T(256)S(1)}, u32[]{:S(2)}, u32[]{:S(2)}) %collective-permute-start.38) | collective-permute-done | bytes 1056 | tf_op jit(solution)/shard_map/ppermute | solution.py:12
  880.8 105.9 %collective-permute-start.46 = (f32[256,256]{0,1:T(8,128)S(1)}, f32[256,256]{0,1:T(8,128)S(1)}, u32[]{:S(2)}, u32[]{:S(2)}) collective-permute-start(f32[256,256]{0,1:T(8,128)S(1)} %fusion.279), channel_id=1, source_target_pairs={{2,0},{3,1},{4,2},{5,3},{6,4},{7,5},{8,6},{9,7},{10,8},{11,9},{12,... | collective-permute-start | bytes 786440 | tf_op jit(solution)/shard_map/ppermute | solution.py:12
  990.0 6.3 collective-permute-done.46
  1027.7 9.0 collective-permute-done.49
  (341 shorter events, 200.7 us)
Async XLA Ops:
  69.6 25.0 %collective-permute-start.10 = (f32[256,256]{0,1:T(8,128)S(1)}, f32[256,256]{0,1:T(8,128)S(1)}, u32[]{:S(2)}, u32[]{:S(2)}) collective-permute-start(f32[256,256]{0,1:T(8,128)S(1)} %copy.142), channel_id=1, source_target_pairs={{0,1},{1,2},{2,3},{3,4},{4,5},{5,6},{6,7},{7,8},{8,9},{9,10},{10,1... | collective-permute-start | bytes 786440 | tf_op jit(solution)/shard_map/ppermute | solution.py:12
  72.0 27.0 %collective-permute-start.6 = (f32[256,256]{0,1:T(8,128)S(1)}, f32[256,256]{0,1:T(8,128)S(1)}, u32[]{:S(2)}, u32[]{:S(2)}) collective-permute-start(f32[256,256]{0,1:T(8,128)S(1)} %fusion.311), channel_id=1, source_target_pairs={{0,1},{1,2},{2,3},{3,4},{4,5},{5,6},{6,7},{7,8},{8,9},{9,10},{10,1... | collective-permute-start | bytes 786440 | tf_op jit(solution)/shard_map/ppermute | solution.py:12
  78.3 27.0 %collective-permute-start.8 = (f32[256]{0:T(256)S(1)}, f32[256]{0:T(256)S(1)}, u32[]{:S(2)}, u32[]{:S(2)}) collective-permute-start(f32[256]{0:T(256)S(1)} %bitcast.928), channel_id=1, source_target_pairs={{0,1},{1,2},{2,3},{3,4},{4,5},{5,6},{6,7},{7,8},{8,9},{9,10},{10,1... | collective-permute-start | bytes 3080 | tf_op jit(solution)/shard_map/ppermute | solution.py:12
  84.6 22.8 %collective-permute-start.4 = (f32[256]{0:T(256)S(1)}, f32[256]{0:T(256)S(1)}, u32[]{:S(2)}, u32[]{:S(2)}) collective-permute-start(f32[256]{0:T(256)S(1)} %bitcast.908), channel_id=1, source_target_pairs={{0,1},{1,2},{2,3},{3,4},{4,5},{5,6},{6,7},{7,8},{8,9},{9,10},{10,1... | collective-permute-start | bytes 3080 | tf_op jit(solution)/shard_map/ppermute | solution.py:12
  94.7 15.4 %collective-permute-start.1 = (f32[]{:T(128)}, f32[]{:T(128)}, u32[]{:S(2)}, u32[]{:S(2)}) collective-permute-start(f32[]{:T(128)} %select_n.418), channel_id=1, source_target_pairs={{0,1},{1,2},{2,3},{3,4},{4,5},{5,6},{6,7},{7,8},{8,9},{9,10},{10,1... | collective-permute-start | bytes 20 | tf_op jit(solution)/shard_map/ppermute | solution.py:12
  127.3 132.1 %collective-permute-start.17 = (f32[256,256]{0,1:T(8,128)S(1)}, f32[256,256]{0,1:T(8,128)S(1)}, u32[]{:S(2)}, u32[]{:S(2)}) collective-permute-start(f32[256,256]{0,1:T(8,128)S(1)} %broadcast_select_fusion.34), channel_id=1, source_target_pairs={{0,2},{1,3},{2,4},{3,5},{4,6},{5,7},{6,8},{7,9},{8,10},{9,11},{10,... | collective-permute-start | bytes 786440 | tf_op jit(solution)/shard_map/ppermute | solution.py:12
  237.9 21.6 %collective-permute-start.15 = (f32[256,256]{0,1:T(8,128)S(1)}, f32[256,256]{0,1:T(8,128)S(1)}, u32[]{:S(2)}, u32[]{:S(2)}) collective-permute-start(f32[256,256]{0,1:T(8,128)S(1)} %broadcast_select_fusion.35), channel_id=1, source_target_pairs={{0,2},{1,3},{2,4},{3,5},{4,6},{5,7},{6,8},{7,9},{8,10},{9,11},{10,... | collective-permute-start | bytes 786440 | tf_op jit(solution)/shard_map/ppermute | solution.py:12
  240.9 18.6 %collective-permute-start.13 = (f32[256,256]{0,1:T(8,128)S(1)}, f32[256,256]{0,1:T(8,128)S(1)}, u32[]{:S(2)}, u32[]{:S(2)}) collective-permute-start(f32[256,256]{0,1:T(8,128)S(1)} %broadcast_select_fusion.36), channel_id=1, source_target_pairs={{0,2},{1,3},{2,4},{3,5},{4,6},{5,7},{6,8},{7,9},{8,10},{9,11},{10,... | collective-permute-start | bytes 786440 | tf_op jit(solution)/shard_map/ppermute | solution.py:12
  275.6 130.9 %collective-permute-start.23 = (f32[256,256]{0,1:T(8,128)S(1)}, f32[256,256]{0,1:T(8,128)S(1)}, u32[]{:S(2)}, u32[]{:S(2)}) collective-permute-start(f32[256,256]{0,1:T(8,128)S(1)} %broadcast_select_fusion.31), channel_id=1, source_target_pairs={{0,4},{1,5},{2,6},{3,7},{4,8},{5,9},{6,10},{7,11},{8,12},{9,13},{1... | collective-permute-start | bytes 786440 | tf_op jit(solution)/shard_map/ppermute | solution.py:12
  384.4 22.1 %collective-permute-start.21 = (f32[256,256]{0,1:T(8,128)S(1)}, f32[256,256]{0,1:T(8,128)S(1)}, u32[]{:S(2)}, u32[]{:S(2)}) collective-permute-start(f32[256,256]{0,1:T(8,128)S(1)} %broadcast_select_fusion.32), channel_id=1, source_target_pairs={{0,4},{1,5},{2,6},{3,7},{4,8},{5,9},{6,10},{7,11},{8,12},{9,13},{1... | collective-permute-start | bytes 786440 | tf_op jit(solution)/shard_map/ppermute | solution.py:12
  390.1 16.4 %collective-permute-start.19 = (f32[256,256]{0,1:T(8,128)S(1)}, f32[256,256]{0,1:T(8,128)S(1)}, u32[]{:S(2)}, u32[]{:S(2)}) collective-permute-start(f32[256,256]{0,1:T(8,128)S(1)} %broadcast_select_fusion.33), channel_id=1, source_target_pairs={{0,4},{1,5},{2,6},{3,7},{4,8},{5,9},{6,10},{7,11},{8,12},{9,13},{1... | collective-permute-start | bytes 786440 | tf_op jit(solution)/shard_map/ppermute | solution.py:12
  422.8 127.3 %collective-permute-start.29 = (f32[256,256]{0,1:T(8,128)S(1)}, f32[256,256]{0,1:T(8,128)S(1)}, u32[]{:S(2)}, u32[]{:S(2)}) collective-permute-start(f32[256,256]{0,1:T(8,128)S(1)} %broadcast_select_fusion.28), channel_id=1, source_target_pairs={{0,8},{1,9},{2,10},{3,11},{4,12},{5,13},{6,14},{7,15},{8,16},{9,17... | collective-permute-start | bytes 786440 | tf_op jit(solution)/shard_map/ppermute | solution.py:12
  531.2 18.9 %collective-permute-start.27 = (f32[256,256]{0,1:T(8,128)S(1)}, f32[256,256]{0,1:T(8,128)S(1)}, u32[]{:S(2)}, u32[]{:S(2)}) collective-permute-start(f32[256,256]{0,1:T(8,128)S(1)} %broadcast_select_fusion.29), channel_id=1, source_target_pairs={{0,8},{1,9},{2,10},{3,11},{4,12},{5,13},{6,14},{7,15},{8,16},{9,17... | collective-permute-start | bytes 786440 | tf_op jit(solution)/shard_map/ppermute | solution.py:12
  535.6 14.5 %collective-permute-start.25 = (f32[256,256]{0,1:T(8,128)S(1)}, f32[256,256]{0,1:T(8,128)S(1)}, u32[]{:S(2)}, u32[]{:S(2)}) collective-permute-start(f32[256,256]{0,1:T(8,128)S(1)} %broadcast_select_fusion.30), channel_id=1, source_target_pairs={{0,8},{1,9},{2,10},{3,11},{4,12},{5,13},{6,14},{7,15},{8,16},{9,17... | collective-permute-start | bytes 786440 | tf_op jit(solution)/shard_map/ppermute | solution.py:12
  563.0 113.5 %collective-permute-start.32 = (f32[256,256]{0,1:T(8,128)S(1)}, f32[256,256]{0,1:T(8,128)S(1)}, u32[]{:S(2)}, u32[]{:S(2)}) collective-permute-start(f32[256,256]{0,1:T(8,128)S(1)} %broadcast_select_fusion.27), channel_id=1, source_target_pairs={{0,16},{1,17},{2,18},{3,19},{4,20},{5,21},{6,22},{7,23},{8,24},{9,... | collective-permute-start | bytes 786440 | tf_op jit(solution)/shard_map/ppermute | solution.py:12
  761.0 108.1 %collective-permute-start.44 = (f32[256,256]{0,1:T(8,128)S(1)}, f32[256,256]{0,1:T(8,128)S(1)}, u32[]{:S(2)}, u32[]{:S(2)}) collective-permute-start(f32[256,256]{0,1:T(8,128)S(1)} %convolution_subtract_fusion.34), channel_id=1, source_target_pairs={{1,0},{2,1},{3,2},{4,3},{5,4},{6,5},{7,6},{8,7},{9,8},{10,9},{11,1... | collective-permute-start | bytes 786440 | tf_op jit(solution)/shard_map/ppermute | solution.py:12
  762.9 104.9 %collective-permute-start.38 = (f32[256]{0:T(256)S(1)}, f32[256]{0:T(256)S(1)}, u32[]{:S(2)}, u32[]{:S(2)}) collective-permute-start(f32[256]{0:T(256)S(1)} %sub.74), channel_id=1, source_target_pairs={{1,0},{2,1},{3,2},{4,3},{5,4},{6,5},{7,6},{8,7},{9,8},{10,9},{11,1... | collective-permute-start | bytes 3080 | tf_op jit(solution)/shard_map/ppermute | solution.py:12
  764.2 106.2 %collective-permute-start.33 = (f32[256,256]{0,1:T(8,128)S(1)}, f32[256,256]{0,1:T(8,128)S(1)}, u32[]{:S(2)}, u32[]{:S(2)}) collective-permute-start(f32[256,256]{0,1:T(8,128)S(1)} %fusion.319), channel_id=1, source_target_pairs={{1,0},{2,1},{3,2},{4,3},{5,4},{6,5},{7,6},{8,7},{9,8},{10,9},{11,1... | collective-permute-start | bytes 786440 | tf_op jit(solution)/shard_map/ppermute | solution.py:12
  870.5 116.2 %collective-permute-start.34 = (f32[256,256]{0,1:T(8,128)S(1)}, f32[256,256]{0,1:T(8,128)S(1)}, u32[]{:S(2)}, u32[]{:S(2)}) collective-permute-start(f32[256,256]{0,1:T(8,128)S(1)} %convert_select_fusion), channel_id=1, source_target_pairs={{1,0},{2,1},{3,2},{4,3},{5,4},{6,5},{7,6},{8,7},{9,8},{10,9},{11,1... | collective-permute-start | bytes 786440 | tf_op jit(solution)/shard_map/ppermute | solution.py:12
  877.5 110.9 %collective-permute-start.40 = (f32[256]{0:T(256)S(1)}, f32[256]{0:T(256)S(1)}, u32[]{:S(2)}, u32[]{:S(2)}) collective-permute-start(f32[256]{0:T(256)S(1)} %add_select_fusion.4), channel_id=1, source_target_pairs={{2,0},{3,1},{4,2},{5,3},{6,4},{7,5},{8,6},{9,7},{10,8},{11,9},{12,... | collective-permute-start | bytes 3080 | tf_op jit(solution)/shard_map/ppermute | solution.py:12
  880.8 115.5 %collective-permute-start.46 = (f32[256,256]{0,1:T(8,128)S(1)}, f32[256,256]{0,1:T(8,128)S(1)}, u32[]{:S(2)}, u32[]{:S(2)}) collective-permute-start(f32[256,256]{0,1:T(8,128)S(1)} %fusion.279), channel_id=1, source_target_pairs={{2,0},{3,1},{4,2},{5,3},{6,4},{7,5},{8,6},{9,7},{10,8},{11,9},{12,... | collective-permute-start | bytes 786440 | tf_op jit(solution)/shard_map/ppermute | solution.py:12
  987.1 14.3 %collective-permute-start.35 = (f32[256,256]{0,1:T(8,128)S(1)}, f32[256,256]{0,1:T(8,128)S(1)}, u32[]{:S(2)}, u32[]{:S(2)}) collective-permute-start(f32[256,256]{0,1:T(8,128)S(1)} %convolution_select_fusion.3), channel_id=1, source_target_pairs={{2,0},{3,1},{4,2},{5,3},{6,4},{7,5},{8,6},{9,7},{10,8},{11,9},{12,... | collective-permute-start | bytes 786440 | tf_op jit(solution)/shard_map/ppermute | solution.py:12
  988.7 14.5 %collective-permute-start.41 = (f32[256]{0:T(256)S(1)}, f32[256]{0:T(256)S(1)}, u32[]{:S(2)}, u32[]{:S(2)}) collective-permute-start(f32[256]{0:T(256)S(1)} %add_select_fusion.3), channel_id=1, source_target_pairs={{4,0},{5,1},{6,2},{7,3},{8,4},{9,5},{10,6},{11,7},{12,8},{13,9},{1... | collective-permute-start | bytes 3080 | tf_op jit(solution)/shard_map/ppermute | solution.py:12
  1021.0 15.7 %collective-permute-start.49 = (f32[256,256]{0,1:T(8,128)S(1)}, f32[256,256]{0,1:T(8,128)S(1)}, u32[]{:S(2)}, u32[]{:S(2)}) collective-permute-start(f32[256,256]{0,1:T(8,128)S(1)} %fusion.276), channel_id=1, source_target_pairs={{16,0},{17,1},{18,2},{19,3},{20,4},{21,5},{22,6},{23,7},{24,8},{25... | collective-permute-start | bytes 786440 | tf_op jit(solution)/shard_map/ppermute | solution.py:12
  (54 other events, 610.5 us)
where the time goes:
time: 1050 us; the launch traced here: 1040 us
  starting transfers between devices  664 us (63%)
  waiting for transfers between devices  139 us (13%)
  other arithmetic  114 us (11%)
  loops' own time  62.4 us (6%)
  local copies, waits for them, and re-layouts  29.1 us (3%)
  matrix products  20.6 us (2%)
    ppermute x50, starting transfers between devices, passed_along(): lax.ppermute(value, axis, [(source, source + steps) for source in range(f...  664 us
    ppermute x50, waiting for transfers between devices, passed_along(): lax.ppermute(value, axis, [(source, source + steps) for source in range(f...  139 us
    another operation x5, loops' own time, fold_filter(): return lax.cond(earlier[0] * later[0] > 0, joined, passed)  53.8 us
    another operation x7, other arithmetic, smooth_element(): factor = jnp.linalg.cholesky(predicted)  34.6 us
    another operation x6, other arithmetic, build_element(): factor = jnp.linalg.cholesky(jnp.diag(prec_diag) + info_dense)  34.1 us
  transfers between devices with their start and end apart: 50, of which 15 were waited for; matrix products, arithmetic and copies ran while one was open for 1% of the time, Pallas kernels for 0%

commit v1 on v0

v1 whole, which is shorter than its diff:
```python
import functools
import jax
import jax.numpy as jnp
from jax import lax
from jax.experimental import pallas as pl
from jax.experimental.pallas import tpu as pltpu
from jax.sharding import PartitionSpec as P

HALF = 128
TILE = 8
MESH = pl.DeviceIdType.MESH


def halves(value):
    high = value.astype(jnp.bfloat16)
    return high, (value - high.astype(jnp.float32)).astype(jnp.bfloat16)


def mm(left, right, dims=((1,), (0,))):
    left_high, left_low = halves(left)
    right_high, right_low = halves(right)
    return lax.dot_general(
        jnp.concatenate([left_low, left_high, left_high], axis=dims[0][0]),
        jnp.concatenate([right_high, right_low, right_high], axis=dims[1][0]),
        (dims, ((), ())),
        preferred_element_type=jnp.float32,
    )


NT = ((1,), (1,))
TN = ((0,), (0,))


def reciprocal(value):
    guess = pl.reciprocal(value, approx=True)
    guess = guess * (2.0 - value * guess)
    return guess * (2.0 - value * guess)


def invert_half(matrix):
    size = matrix.shape[0]
    lane = lax.broadcasted_iota(jnp.int32, (TILE, size), 1)
    row = lax.broadcasted_iota(jnp.int32, (TILE, size), 0)
    lane_all = lax.broadcasted_iota(jnp.int32, (1, size), 1)
    pivots = [
        jnp.broadcast_to(matrix[:TILE, j : j + 1], (TILE, size)) for j in range(TILE)
    ]
    for first in range(0, size, TILE):
        last = first + TILE
        more = range(last, min(last + TILE, size))
        wide = [
            jnp.broadcast_to(matrix[:, first + j : first + j + 1], (size, size))
            for j in range(TILE)
        ]
        beside = [jnp.broadcast_to(matrix[first:last, m : m + 1], (TILE, size)) for m in more]
        ahead = [
            jnp.broadcast_to(matrix[last : last + TILE, m : m + 1], (TILE, size)) for m in more
        ]
        inside = (lane >= first) & (lane < last)
        rows = jnp.where(inside, (lane - first == row).astype(jnp.float32), matrix[first:last])
        for j in range(0, TILE, 2):
            k = j + 1
            own = (row == j) | (row == k)
            a, b = (pivots[j][j : j + 1], pivots[k][j : j + 1])
            c, d = (pivots[j][k : k + 1], pivots[k][k : k + 1])
            scale = reciprocal(a * d - b * c)
            factor_j = jnp.where(own, jnp.where(row == j, -1.0, 0.0), pivots[j])
            factor_k = jnp.where(own, jnp.where(row == k, -1.0, 0.0), pivots[k])

            def swept(part):
                at_j, at_k = (part[j : j + 1], part[k : k + 1])
                new_j = (d * at_j - b * at_k) * scale
                new_k = (a * at_k - c * at_j) * scale
                return jnp.where(own, 0.0, part) - (factor_j * new_j + factor_k * new_k)

            pivots = pivots[: j + 2] + [swept(part) for part in pivots[j + 2 :]]
            beside = [swept(part) for part in beside]
            rows = swept(rows)

        def taken(start, columns, factors):
            pairs = [
                columns[j] * factors[j : j + 1] + columns[j + 1] * factors[j + 1 : j + 2]
                for j in range(0, TILE, 2)
            ]
            return start - ((pairs[0] + pairs[1]) + (pairs[2] + pairs[3]))

        pivots = [
            taken(old, [column[last : last + TILE] for column in wide], part)
            for old, part in zip(ahead, beside)
        ]
        kept = (lane_all < first) | (lane_all >= last)
        rest = taken(jnp.where(kept, matrix, 0.0), wide, rows)
        pieces = [rest[:first], rows, rest[last:]]
        matrix = jnp.concatenate([piece for piece in pieces if piece.shape[0]], axis=0)
    return matrix


def invert(matrix):
    size = matrix.shape[0]
    same = lax.broadcasted_iota(jnp.int32, (size, size), 0) == lax.broadcasted_iota(
        jnp.int32, (size, size), 1
    )
    diagonal = jnp.max(jnp.where(same, matrix, 0.0), axis=0, keepdims=True)
    unit = 1.0 / jnp.max(diagonal, axis=1, keepdims=True)
    matrix = matrix * unit
    side = matrix[:HALF, HALF:]
    top_first = invert_half(matrix[:HALF, :HALF])
    turned = mm(top_first, side)
    low_inverse = invert_half(matrix[HALF:, HALF:] - mm(side, turned, TN)) * unit
    across = mm(turned, low_inverse)
    top_inverse = top_first * unit + mm(across, turned, NT)
    return jnp.concatenate(
        [
            jnp.concatenate([top_inverse, -across], axis=1),
            jnp.concatenate([-across.T, low_inverse], axis=1),
        ],
        axis=0,
    )


def kernel(
    devices, rounds, transition, noise_var, prior_mean, prior_var, obs_op, obs_value, obs_noise,
    obs_block, obs_count, mean_out, var_out, cov, prec, lin, info, off, vec, step_lin,
    send_v, send_w, send_k, recv_v, recv_w, recv_k, sent, landed,
):
    size = transition.shape[0]
    slots, stations, width = obs_op.shape[1:]
    nblocks = size // width
    me = lax.axis_index("tm")

    barrier = pltpu.get_barrier_semaphore()
    for level in range(rounds):
        step = 1 << level

        @pl.when(me + step < devices)
        def _():
            pl.semaphore_signal(barrier, inc=1, device_id=(me + step,), device_id_type=MESH)

        @pl.when(me >= step)
        def _():
            pl.semaphore_signal(barrier, inc=1, device_id=(me - step,), device_id_type=MESH)

    noise = obs_noise[0]
    noise_cols = noise.T
    weighted = obs_value[0] / noise
    slot_row = lax.broadcasted_iota(jnp.int32, (TILE, stations), 0)
    scaled_slots, weight_slots, op_slots = ([], [], [])
    for m in range(slots):
        used = m < obs_count[0]
        block = obs_block[0, m]
        op = obs_op[0, m]
        scaled = (op.astype(jnp.float32) / noise_cols[:, m : m + 1]).astype(jnp.bfloat16)
        picks = [
            jnp.where(used & (block == a), 1.0, 0.0).astype(jnp.float32) for a in range(nblocks)
        ]
        wide = scaled.astype(jnp.float32)
        scaled_slots.append(
            jnp.concatenate([(wide * pick).astype(jnp.bfloat16) for pick in picks], axis=1)
        )
        row_weight = jnp.zeros((TILE, stations), jnp.float32)
        for a, pick in enumerate(picks):
            row_weight = row_weight + jnp.where(slot_row == a, weighted[m : m + 1] * pick, 0.0)
        weight_slots.append(row_weight)
        op_slots.append(op)
    ops = jnp.concatenate(op_slots, axis=0)
    stacked = lax.dot_general(
        jnp.concatenate(scaled_slots, axis=0),
        ops,
        (TN, ((), ())),
        preferred_element_type=jnp.float32,
    )
    shifts = mm(jnp.concatenate(weight_slots, axis=1), ops.astype(jnp.float32))
    blank = jnp.zeros((width, width), jnp.float32)
    info[...] = jnp.concatenate(
        [
            jnp.concatenate(
                [
                    stacked[a * width : (a + 1) * width] if a == c else blank
                    for c in range(nblocks)
                ],
                axis=1,
            )
            for a in range(nblocks)
        ],
        axis=0,
    )
    first_row = lax.broadcasted_iota(jnp.int32, (TILE, size), 0) == 0
    shift_row = jnp.concatenate([shifts[a : a + 1] for a in range(nblocks)], axis=1)
    vec[...] = jnp.where(first_row, shift_row, 0.0)

    start = me == 0
    same = lax.broadcasted_iota(jnp.int32, (size, size), 0) == lax.broadcasted_iota(
        jnp.int32, (size, size), 1
    )
    variance = jnp.where(start, prior_var[...], noise_var[...])
    cov[...] = jnp.where(same, variance, 0.0)
    prec[...] = jnp.where(same, 1.0 / variance, 0.0)
    moving = jnp.where(start, 0.0, 1.0).astype(jnp.float32)
    lin[...] = transition[...] * moving
    step_lin[...] = jnp.zeros_like(step_lin)
    off[...] = jnp.where(first_row, prior_mean[...] * (1.0 - moving), 0.0)

    peers = jnp.int32(0)
    for level in range(rounds):
        step = 1 << level
        peers = peers + jnp.where(me + step < devices, 1, 0) + jnp.where(me >= step, 1, 0)
    pl.semaphore_wait(barrier, peers)

    def copies(level, step):
        def one(source, target, kind, to):
            return pltpu.make_async_remote_copy(
                src_ref=source.at[level],
                dst_ref=target.at[level],
                send_sem=sent.at[level, kind],
                recv_sem=landed.at[level, kind],
                device_id=(to,),
                device_id_type=MESH,
            )

        return (
            one(send_v, recv_v, 0, me + step),
            one(send_w, recv_w, 1, me + step),
            one(send_k, recv_k, 2, me - step),
        )

    def turn(level, step):
        longer = (level > 0) & (me >= step // 2)
        link = jnp.where(longer, mm(lin[...], step_lin[...]), lin[...])
        lin[...] = link
        weighed = mm(prec[...], link)
        seen = mm(info[...], link)
        joint = invert(prec[...] + info[...])
        state = mm(vec[...] + mm(off[...], prec[...]), joint)
        copy_v, copy_w, copy_k = copies(level, step)
        right = me + step < devices
        left = me >= step

        @pl.when(level == rounds)
        def _():
            mean_out[...] = state[:1]
            var_out[...] = jnp.sum(jnp.where(same, joint, 0.0), axis=0, keepdims=True)

        @pl.when(level < rounds)
        def _():
            @pl.when(right)
            def _():
                send_v[level, :size] = joint
                send_v[level, size:] = state
                copy_v.start()

            passed = mm(joint, weighed)
            send_w[level] = passed
            send_k[level, :size] = mm(passed, seen, TN)
            send_k[level, size:] = mm(vec[...] - mm(off[...], info[...]), passed)

            @pl.when(left)
            def _():
                copy_v.wait_recv()
                copy_k.start()

            @pl.when(right)
            def _():
                copy_w.start()

            @pl.when(left)
            def _():
                spread = mm(lin[...], recv_v[level, :size])
                cov[...] = cov[...] + mm(spread, lin[...], NT)
                off[...] = off[...] + mm(recv_v[level, size:], lin[...], NT)

            prec[...] = invert(cov[...])

            @pl.when(left)
            def _():
                copy_w.wait_recv()
                step_lin[...] = recv_w[level]
                copy_k.wait_send()

            @pl.when(right)
            def _():
                copy_k.wait_recv()
                info[...] = info[...] + recv_k[level, :size]
                vec[...] = vec[...] + recv_k[level, size:]
                copy_v.wait_send()
                copy_w.wait_send()

        return step * 2

    lax.fori_loop(0, rounds + 1, turn, 1)


def local(
    transition, noise_var, prior_mean, prior_var, obs_op, obs_value, obs_noise, obs_block, obs_count
):
    devices = lax.axis_size("tm")
    size = transition.shape[0]
    rounds = (devices - 1).bit_length()
    slots = max(rounds, 1)
    vmem = pl.BlockSpec(memory_space=pltpu.VMEM)
    smem = pl.BlockSpec(memory_space=pltpu.SMEM)
    square = pltpu.VMEM((size, size), jnp.float32)
    rows = pltpu.VMEM((TILE, size), jnp.float32)
    tall = pltpu.VMEM((slots, size + TILE, size), jnp.float32)
    flat = pltpu.VMEM((slots, size, size), jnp.float32)
    row = jax.ShapeDtypeStruct((1, size), jnp.float32)
    return pl.pallas_call(
        functools.partial(kernel, devices, rounds),
        out_shape=(row, row),
        in_specs=[vmem] * 7 + [smem] * 2,
        out_specs=(vmem, vmem),
        scratch_shapes=[
            square, square, square, square, rows, rows,
            square,
            tall, flat, tall, tall, flat, tall,
            pltpu.SemaphoreType.DMA((slots, 3)),
            pltpu.SemaphoreType.DMA((slots, 3)),
        ],
        compiler_params=pltpu.CompilerParams(
            collective_id=0, has_side_effects=True, vmem_limit_bytes=40 * 1024 * 1024
        ),
    )(
        transition,
        noise_var[None],
        prior_mean[None],
        prior_var[None],
        obs_op,
        obs_value,
        obs_noise,
        obs_block,
        obs_count,
    )


def solution(mesh):
    return jax.shard_map(
        local,
        mesh=mesh,
        in_specs=(
            P(),
            P(),
            P(),
            P(),
            P("tm", None, None, None),
            P("tm", None, None),
            P("tm", None, None),
            P("tm", None),
            P("tm"),
        ),
        out_specs=(P("tm", None), P("tm", None)),
        check_vma=False,
    )
```

time: 1050 us -> 163 us (0.16)
  the two profiles are of different devices: /device:TPU:0 before, /device:TPU:31 now
where the time goes in v1:
time: 163 us
  Pallas kernels  157 us (96%)
  local copies, waits for them, and re-layouts  4.39 us (3%)
    pallas_call x1, Pallas kernels, local(): pl.pallas_call(functools.partial(kernel, devices, rounds), out_shape=(row...  157 us
    unnamed x18, local copies, waits for them, and re-layouts  4.39 us

profile of v1, /device:TPU:31, one launch (start us, length us, event | category | flops | bytes accessed | tf_op | source)
XLA Modules:
  0.0 163.1 jit_solution(8520984311825999213)
XLA Ops:
  0.6 0.0 copy-start.2
  1.3 0.0 copy-start.5
  1.3 0.0 copy-start.6
  1.3 0.0 copy-start.4
  1.3 0.0 copy-start.7
  1.3 0.0 copy-done.2
  1.4 0.6 copy-done.5
  2.0 0.0 copy-done.6
  2.0 0.0 copy-done.4
  2.0 0.0 copy-done.7
  2.0 0.0 copy-start
  2.0 0.9 copy-done
  3.0 0.0 copy-start.1
  3.0 0.9 copy-done.1
  3.9 0.0 copy-start.3
  3.9 0.7 copy-done.3
  4.6 157.4 %shard_map.104 = (f32[1,256]{1,0:T(1,128)S(1)}, f32[1,256]{1,0:T(1,128)S(1)}) custom-call(f32[256,256]{1,0:T(8,128)S(1)} %copy-done, f32[1,256]{1,0:T(1,128)S(1)} %bitcast.3, f32[1,256]{1,0:T(1,128)S(1)} %bitcast.4, f32[1,256]{1,0:T(1,128)S(1)} %bitcast.5, bf16[1,8,128,128]{3,2,1,0:T(8,128)(2,1)S(1)} %copy-done.1, f32[1,8,128]{2,1,0:T(8,128)S(1)} %copy-done.2, ...), custom_call_target="tpu_custom_call" | custom-call | tf_op jit(solution)/shard_map/pallas_call | solution.py:306
  162.0 0.6 copy.14
  162.5 0.6 copy.15
Async XLA Ops:
  0.6 0.7 copy-start.2
  1.3 0.7 copy-start.5
  1.3 0.7 copy-start.6
  1.3 0.7 copy-start.4
  1.3 0.7 copy-start.7
  2.0 1.0 copy-start
  3.0 0.9 copy-start.1
  3.9 0.7 copy-start.3
